TPU v7x, 512 devices: a whole 4x4x16 slice. The times are simulated.
512 devices in a mesh: rx: 32 (over z_lo, x), tx: 16 (over y, z_hi, core).
Axes of the slice: x: 4, y: 4, z: 16 (z_hi: 2, z_lo: 8; z = z_hi * 8 + z_lo), core: 2. Of those that a mesh axis runs over, the one named last changes fastest.
Arguments:
- sender_xy: int32 [2, 32768], P(None, ('tx', 'rx')), may hold values from 0 to 255, as said below
- listener_xy: int32 [2, 32768], P(None, ('rx', 'tx')), may hold values from 0 to 256, as said below
- powers: float32 [32768, 128], P(('tx', 'rx')), may hold values from 0.25 to 1
- weight: int32 [32768], P(('rx', 'tx')), may hold values from 1 to 16
- fairness: int32 [32768], P(('rx', 'tx')), may hold values from 0 to 2
- step_code: int32 [1], replicated, may hold values from 256 to 4096
Outputs:
- quality: float32 [32768, 128], P(('rx', 'tx'))
- gradient: float32 [32768, 128], P(('tx', 'rx'))
- new_power: float32 [32768, 128], P(('tx', 'rx'))
- duality_gap: float32 [1], replicated
Inputs may be any that keep to these rules, and one draw needn't show every extreme that they name: `sender_xy`: row 0 lies in 0 to 255 and row 1 in 0 to 255. `listener_xy`: each entry equals the sender_xy entry of the same user or exceeds it by one.
All inputs are finite; a program needn't handle non-finite values.
Results may differ from a plain program's by a relative error of at most 0.0003.
Values sent between devices are 32-bit elements; how exact they have to be, the bound alone decides.
No kernel may reach another device: no remote copies, remote signals or barrier semaphores. Data moves between devices by JAX's collectives and lax.ppermute only.
A program may use at most 64 MiB of HBM per device.

v0:
```python
import jax
import jax.numpy as jnp
from jax import lax
from jax.sharding import PartitionSpec as P

NOISE_POWER = 0.05
ARRAY_GAIN = 32.0
WEIGHT_UNIT = 1.0 / 16.0
PEAK_POWER = 1.0


def path_gain(listen, sender):
    delta_x = listen[0].astype(jnp.float32)[:, None] - sender[0].astype(jnp.float32)[None, :]
    delta_y = listen[1].astype(jnp.float32)[:, None] - sender[1].astype(jnp.float32)[None, :]
    return 1.0 / (1.0 + delta_x * delta_x + delta_y * delta_y)


def derivatives(interference, signal, user_weight, user_fair):
    denominator = NOISE_POWER + interference
    quality = signal / denominator
    user_scale = WEIGHT_UNIT * user_weight.astype(jnp.float32)
    marginal = (
        user_scale[:, None]
        * jnp.exp(-user_fair.astype(jnp.float32)[:, None] * jnp.log(quality))
        / denominator
    )
    return (quality, marginal, marginal * quality)


def per_device(sender_xy, listener_xy, powers, weight, fairness, step_code):
    rx_here = lax.axis_index("rx")
    tx_here = lax.axis_index("tx")
    user_rows = powers.shape[0]
    channels = powers.shape[1]
    senders, sender_power = (
        lax.all_gather(sender_xy, "rx", axis=1, tiled=True),
        lax.all_gather(powers, "rx", axis=0, tiled=True),
    )
    listeners = lax.all_gather(listener_xy, "tx", axis=1, tiled=True)
    rx_width = listeners.shape[1]
    tx_width = senders.shape[1]
    row_start = rx_here * rx_width
    col_start = tx_here * tx_width
    gain_tile = path_gain(listeners, senders)
    row_ids = row_start + jnp.arange(rx_width, dtype=jnp.int32)
    col_ids = col_start + jnp.arange(tx_width, dtype=jnp.int32)
    diagonal = row_ids[:, None] == col_ids[None, :]
    crossing = jnp.where(diagonal, 0.0, gain_tile)
    own_gain = jnp.sum(jnp.where(diagonal, gain_tile, 0.0), axis=1)
    offset = row_start % tx_width
    interference_part = jnp.dot(crossing, sender_power, precision=lax.Precision.HIGHEST)
    signal_part = (
        ARRAY_GAIN * own_gain[:, None] * lax.dynamic_slice_in_dim(sender_power, offset, rx_width, 0)
    )
    interference, signal = (
        lax.psum_scatter(interference_part, "tx", scatter_dimension=0, tiled=True),
        lax.psum_scatter(signal_part, "tx", scatter_dimension=0, tiled=True),
    )
    quality, marginal, pressure = derivatives(interference, signal, weight, fairness)
    marginal_all, pressure_all = (
        lax.all_gather(marginal, "tx", axis=0, tiled=True),
        lax.all_gather(pressure, "tx", axis=0, tiled=True),
    )
    own_term = ARRAY_GAIN * own_gain[:, None] * marginal_all
    own_full = lax.dynamic_update_slice_in_dim(
        jnp.zeros((tx_width, channels), jnp.float32), own_term, offset, 0
    )
    pushed = lax.dot_general(
        crossing, pressure_all, (((0,), (0,)), ((), ())), precision=lax.Precision.HIGHEST
    )
    totals = lax.psum(own_full - pushed, "rx")
    gradient = lax.dynamic_slice_in_dim(totals, rx_here * user_rows, user_rows, 0)
    target = PEAK_POWER * jax.nn.sigmoid(gradient)
    step_size = step_code[0].astype(jnp.float32) / 4096.0
    new_power = powers + step_size * (target - powers)
    gap_local = jnp.sum(PEAK_POWER * jnp.maximum(gradient, 0.0) - gradient * powers)
    gap_sum = lax.psum(gap_local, ("rx", "tx"))
    duality_gap = (
        gap_sum / (user_rows * channels * lax.axis_size("rx") * lax.axis_size("tx"))
    ).reshape(1)
    return (quality, gradient, new_power, duality_gap)


def solution(mesh):
    placed = (
        P(None, ("tx", "rx")),
        P(None, ("rx", "tx")),
        P(("tx", "rx"), None),
        P(("rx", "tx")),
        P(("rx", "tx")),
        P(),
    )
    return jax.shard_map(
        per_device,
        mesh=mesh,
        in_specs=placed,
        out_specs=(P(("rx", "tx"), None), P(("tx", "rx"), None), P(("tx", "rx"), None), P()),
        check_vma=False,
    )
```

profile of v0, /device:TPU:1, one launch (start us, length us, event | category | flops | bytes accessed | tf_op | source)
XLA Modules:
  0.0 1118.0 jit_solution(16016938262697707755)
XLA Ops:
  7.2 0.7 all-gather.4.cloned.1.call-update
  7.9 0.0 reduce-scatter.3.cloned.1.call-start
  8.0 51.2 %all-gather = s32[16,64,2]{1,2,0:T(2,128)S(1)} all-gather(s32[1,64,2]{1,2,0:T(2,128)} %bitcast.34), channel_id=1, replica_groups=mesh['rx'=32,'tx'=16] {'tx'}, dimensions={0}, use_global_device_ids=true | all-gather | bytes 8704 | tf_op jit(solution)/shard_map/all_gather | solution.py:39
  59.1 0.1 reshape.43
  59.3 104.0 %all-gather.1 = s32[32,64,2]{1,2,0:T(2,128)S(1)} all-gather(s32[1,64,2]{1,2,0:T(2,128)} %bitcast.35), channel_id=1, replica_groups=mesh['rx'=32,'tx'=16] {'rx'}, dimensions={0}, use_global_device_ids=true | all-gather | bytes 16896 | tf_op jit(solution)/shard_map/all_gather | solution.py:36
  163.3 0.1 reshape.45
  163.5 3.1 fusion
  166.5 49.7 %all-gather.4.cloned.1.call-done = f32[2048,128]{1,0:T(8,128)} async-done(((f32[64,128]{1,0:T(8,128)}), f32[2048,128]{1,0:T(8,128)}) %all-gather.4.cloned.1.call-update) | async-done | bytes 1048592 | tf_op jit(solution)/shard_map/all_gather | solution.py:37
  216.2 2.1 dynamic-slice_multiply_fusion
  218.4 0.0 reduce-scatter.5.cloned.1.call-start
  218.5 9.3 fusion.2
  227.8 0.0 all-reduce.2.cloned.1.call-start
  227.9 111.3 %reduce-scatter.3.cloned.1.call-done = f32[64,128]{1,0:T(8,128)} async-done(((f32[1024,128]{1,0:T(8,128)}), f32[64,128]{1,0:T(8,128)}) %reduce-scatter.3.cloned.1.call-update) | async-done | bytes 32784 | tf_op jit(solution)/shard_map/reduce_scatter | solution.py:57
  339.2 96.6 %reduce-scatter.5.cloned.1.call-done = f32[64,128]{1,0:T(8,128)} async-done(((f32[1024,128]{1,0:T(8,128)}), f32[64,128]{1,0:T(8,128)}) %reduce-scatter.5.cloned.1.call-update) | async-done | bytes 32784 | tf_op jit(solution)/shard_map/reduce_scatter | solution.py:56
  435.8 1.4 fusion.14
  437.2 43.2 %all_gather.18 = f32[1024,128]{1,0:T(8,128)S(1)} all-gather(f32[64,128]{1,0:T(8,128)S(1)} %get-tuple-element.7), channel_id=1, replica_groups=mesh['rx'=32,'tx'=16] {'tx'}, dimensions={0}, use_global_device_ids=true | all-gather | bytes 557056 | tf_op jit(solution)/shard_map/all_gather | solution.py:61
  480.4 49.4 %all_gather.19 = f32[1024,128]{1,0:T(8,128)S(1)} all-gather(f32[64,128]{1,0:T(8,128)S(1)} %get-tuple-element.6), channel_id=1, replica_groups=mesh['rx'=32,'tx'=16] {'tx'}, dimensions={0}, use_global_device_ids=true | all-gather | bytes 557056 | tf_op jit(solution)/shard_map/all_gather | solution.py:62
  529.7 0.1 broadcast_in_dim.7
  529.8 0.2 multiply_dynamic-update-slice_fusion
  530.0 16.3 %fusion.9 = f32[2048,128]{1,0:T(8,128)} fusion(f32[2048,128]{1,0:T(8,128)S(1)} %multiply_dynamic-update-slice_fusion, f32[1024,128]{1,0:T(8,128)S(1)} %all_gather.19, f32[2048]{0:T(1024)S(1)} %bitcast.27, f32[1024]{0:T(1024)S(1)} %bitcast.33, f32[2048]{0:T(1024)S(1)} %bitcast.24, f32[1024]{0:T(1024)S(1)} %bitcast.30, s32[2048]{0:T(1024)S(1)} %iota_add_fusion, ...), kind=kOutput, calls=%fused_computation.12 | convolution fusion | flops 3240361984 | bytes 2658304 | tf_op jit(solution)/shard_map/dot_general | solution.py:68
  547.0 437.2 %all-reduce.2.cloned.1.call-done = f32[2048,128]{1,0:T(8,128)} async-done(((f32[2048,128]{1,0:T(8,128)}), f32[2048,128]{1,0:T(8,128)}) %all-reduce.2.cloned.1.call-update) | async-done | bytes 1048592 | tf_op jit(solution)/shard_map/psum | solution.py:71
  984.1 1.4 subtract_reduce_fusion
  985.5 123.6 %psum.15 = f32[]{:T(128)} all-reduce(f32[]{:T(128)} %get-tuple-element.4), channel_id=1, replica_groups=mesh['rx'=32,'tx'=16] {'rx','tx'}, use_global_device_ids=true, to_apply=%region_5.6 | all-reduce | flops 1 | bytes 8 | tf_op jit(solution)/shard_map/psum | solution.py:77
  1109.1 0.6 multiply_add_fusion
  (22 shorter events, 0.2 us)
Async XLA Ops:
  7.2 209.1 %all-gather.4.cloned.1.call-start = ((), (), s32[]{:S(2)}) async-start(), calls=%async_computation.2 | async-start | bytes 1081344 | tf_op jit(solution)/shard_map/all_gather | solution.py:37
  7.9 331.3 %reduce-scatter.3.cloned.1.call-start = ((), (), s32[]{:S(2)}) async-start(), calls=%async_computation.3 | async-start | bytes 557056 | tf_op jit(solution)/shard_map/reduce_scatter | solution.py:57
  216.2 2.2 copy-start.1
  218.4 9.5 copy-start.3
  218.4 9.5 copy-start.4
  218.4 217.4 %reduce-scatter.5.cloned.1.call-start = ((), (), s32[]{:S(2)}) async-start(), calls=%async_computation.4 | async-start | bytes 557056 | tf_op jit(solution)/shard_map/reduce_scatter | solution.py:56
  227.8 756.3 %all-reduce.2.cloned.1.call-start = ((), (), s32[]{:S(2)}) async-start(), calls=%async_computation.5 | async-start | bytes 2097152 | tf_op jit(solution)/shard_map/psum | solution.py:71
  546.3 437.8 %copy-start = (f32[64,128]{1,0:T(8,128)S(1)}, f32[64,128]{1,0:T(8,128)}, u32[]{:S(2)}) copy-start(f32[64,128]{1,0:T(8,128)} %param.8) | copy-start | bytes 98308
  985.5 124.9 %copy-start.2 = (f32[64,128]{1,0:T(8,128)}, f32[64,128]{1,0:T(8,128)S(1)}, u32[]{:S(2)}) copy-start(f32[64,128]{1,0:T(8,128)S(1)} %get-tuple-element.5) | copy-start | bytes 98308
Sparse Core Ops, SparseCore 0:
  10.1 206.1 all-gather.3
  220.9 118.3 reduce-scatter.2
  344.6 91.1 reduce-scatter.4
  546.4 437.6 all-reduce.1
where the time goes:
time: 1120 us
  waiting for transfers between devices  695 us (62%)
  blocking collectives  371 us (33%)
  matrix products  25.6 us (2%)
  between operations  16.3 us (1%)
    psum x1, waiting for transfers between devices, per_device(): totals = lax.psum(own_full - pushed, 'rx')  437 us
    psum x1, blocking collectives, per_device(): gap_sum = lax.psum(gap_local, ('rx', 'tx'))  124 us
    reduce_scatter x1, waiting for transfers between devices, per_device(): lax.psum_scatter(signal_part, 'tx', scatter_dimension=0, tiled=True)  111 us
    all_gather x1, blocking collectives, per_device(): lax.all_gather(sender_xy, 'rx', axis=1, tiled=True)  104 us
    reduce_scatter x1, waiting for transfers between devices, per_device(): lax.psum_scatter(interference_part, 'tx', scatter_dimension=0, tiled=True)  96.6 us
    all_gather x1, blocking collectives, per_device(): listeners = lax.all_gather(listener_xy, 'tx', axis=1, tiled=True)  51.2 us
    all_gather x1, waiting for transfers between devices, per_device(): lax.all_gather(powers, 'rx', axis=0, tiled=True)  49.7 us
    all_gather x1, blocking collectives, per_device(): lax.all_gather(pressure, 'tx', axis=0, tiled=True)  49.4 us
  transfers between devices with their start and end apart: 4, of which 4 were waited for; matrix products, arithmetic and copies ran while one was open for 1% of the time, Pallas kernels for 0%

commit v1 on v0

--- a/solution.py
+++ b/solution.py
@@ -59,7 +59,9 @@
     quality, marginal, pressure = derivatives(interference, signal, weight, fairness)
     marginal_all, pressure_all = (
         lax.all_gather(marginal, "tx", axis=0, tiled=True),
-        lax.all_gather(pressure, "tx", axis=0, tiled=True),
+        jnp.concatenate(
+            lax.all_to_all(jnp.stack([pressure] * lax.axis_size("tx")), "tx", 0, 0), axis=0
+        ),
     )
     own_term = ARRAY_GAIN * own_gain[:, None] * marginal_all
     own_full = lax.dynamic_update_slice_in_dim(

time: 1120 us -> 1100 us (0.982)
  blocking collectives: 371 us -> 342 us
    all_gather x1 -> x0, blocking collectives: 49.4 us -> none  [per_device(): lax.all_gather(pressure, 'tx', axis=0, tiled=True)]
    all_gather x1, blocking collectives: 43.2 us -> 63 us  [per_device(): lax.all_gather(marginal, 'tx', axis=0, tiled=True)]
  transfers between devices with their start and end apart: 4 -> 5, of which waited for: 4 -> 4; matrix products, arithmetic and copies ran while one was open for 1% -> 1% of each run, Pallas kernels for 0% -> 0%
where the time goes in v1:
time: 1100 us
  waiting for transfers between devices  699 us (64%)
  blocking collectives  342 us (31%)
  matrix products  25.6 us (2%)
  between operations  16.3 us (1%)
    psum x1, waiting for transfers between devices, per_device(): totals = lax.psum(own_full - pushed, 'rx')  440 us
    psum x1, blocking collectives, per_device(): gap_sum = lax.psum(gap_local, ('rx', 'tx'))  124 us
    reduce_scatter x1, waiting for transfers between devices, per_device(): lax.psum_scatter(signal_part, 'tx', scatter_dimension=0, tiled=True)  111 us
    all_gather x1, blocking collectives, per_device(): lax.all_gather(sender_xy, 'rx', axis=1, tiled=True)  104 us
    reduce_scatter x1, waiting for transfers between devices, per_device(): lax.psum_scatter(interference_part, 'tx', scatter_dimension=0, tiled=True)  96.6 us
    all_gather x1, blocking collectives, per_device(): lax.all_gather(marginal, 'tx', axis=0, tiled=True)  63 us
    all_gather x1, blocking collectives, per_device(): listeners = lax.all_gather(listener_xy, 'tx', axis=1, tiled=True)  51.2 us
    all_gather x1, waiting for transfers between devices, per_device(): lax.all_gather(powers, 'rx', axis=0, tiled=True)  49.7 us
  transfers between devices with their start and end apart: 5, of which 4 were waited for; matrix products, arithmetic and copies ran while one was open for 1% of the time, Pallas kernels for 0%

profile of v1, /device:TPU:1, one launch (start us, length us, event | category | flops | bytes accessed | tf_op | source)
XLA Modules:
  0.0 1098.6 jit_solution(9321447099170479233)
XLA Ops:
  7.2 0.7 all-gather.4.cloned.1.call-update
  7.9 0.0 reduce-scatter.3.cloned.1.call-start
  8.0 51.2 %all-gather = s32[16,64,2]{1,2,0:T(2,128)S(1)} all-gather(s32[1,64,2]{1,2,0:T(2,128)} %bitcast.36), channel_id=1, replica_groups=mesh['rx'=32,'tx'=16] {'tx'}, dimensions={0}, use_global_device_ids=true | all-gather | bytes 8704 | tf_op jit(solution)/shard_map/all_gather | solution.py:39
  59.1 0.1 reshape.49
  59.3 104.0 %all-gather.1 = s32[32,64,2]{1,2,0:T(2,128)S(1)} all-gather(s32[1,64,2]{1,2,0:T(2,128)} %bitcast.37), channel_id=1, replica_groups=mesh['rx'=32,'tx'=16] {'rx'}, dimensions={0}, use_global_device_ids=true | all-gather | bytes 16896 | tf_op jit(solution)/shard_map/all_gather | solution.py:36
  163.3 0.1 reshape.51
  163.5 3.1 fusion
  166.5 49.7 %all-gather.4.cloned.1.call-done = f32[2048,128]{1,0:T(8,128)} async-done(((f32[64,128]{1,0:T(8,128)}), f32[2048,128]{1,0:T(8,128)}) %all-gather.4.cloned.1.call-update) | async-done | bytes 1048592 | tf_op jit(solution)/shard_map/all_gather | solution.py:37
  216.2 2.1 dynamic-slice_multiply_fusion
  218.4 0.0 reduce-scatter.5.cloned.1.call-start
  218.5 9.3 fusion.2
  227.8 111.4 %reduce-scatter.3.cloned.1.call-done = f32[64,128]{1,0:T(8,128)} async-done(((f32[1024,128]{1,0:T(8,128)}), f32[64,128]{1,0:T(8,128)}) %reduce-scatter.3.cloned.1.call-update) | async-done | bytes 32784 | tf_op jit(solution)/shard_map/reduce_scatter | solution.py:57
  339.2 96.6 %reduce-scatter.5.cloned.1.call-done = f32[64,128]{1,0:T(8,128)} async-done(((f32[1024,128]{1,0:T(8,128)}), f32[64,128]{1,0:T(8,128)}) %reduce-scatter.5.cloned.1.call-update) | async-done | bytes 32784 | tf_op jit(solution)/shard_map/reduce_scatter | solution.py:56
  435.8 1.4 fusion.14
  437.2 0.8 stack.2
  438.0 6.0 all-to-all-start
  444.1 63.0 %all_gather.15 = f32[1024,128]{1,0:T(8,128)S(1)} all-gather(f32[64,128]{1,0:T(8,128)S(1)} %get-tuple-element.7), channel_id=1, replica_groups=mesh['rx'=32,'tx'=16] {'tx'}, dimensions={0}, use_global_device_ids=true | all-gather | bytes 557056 | tf_op jit(solution)/shard_map/all_gather | solution.py:61
  507.1 0.1 broadcast_in_dim.7
  507.2 0.2 multiply_dynamic-update-slice_fusion
  507.4 16.3 %fusion.9 = f32[2048,128]{1,0:T(8,128)} fusion(f32[2048,128]{1,0:T(8,128)S(1)} %multiply_dynamic-update-slice_fusion, f32[1024,128]{1,0:T(8,128)S(1)} %bitcast.21, f32[2048]{0:T(1024)S(1)} %bitcast.29, f32[1024]{0:T(1024)S(1)} %bitcast.35, f32[2048]{0:T(1024)S(1)} %bitcast.26, f32[1024]{0:T(1024)S(1)} %bitcast.32, s32[2048]{0:T(1024)S(1)} %iota_add_fusion, ...), kind=kOutput, calls=%fused_computation.12 | convolution fusion | flops 3240361984 | bytes 2658304 | tf_op jit(solution)/shard_map/dot_general | solution.py:70
  524.4 440.3 %all-reduce.2.cloned.1.call-done = f32[2048,128]{1,0:T(8,128)} async-done(((f32[2048,128]{1,0:T(8,128)}), f32[2048,128]{1,0:T(8,128)}) %all-reduce.2.cloned.1.call-update) | async-done | bytes 1048592 | tf_op jit(solution)/shard_map/psum | solution.py:73
  964.7 1.4 subtract_reduce_fusion
  966.0 123.6 %psum.15 = f32[]{:T(128)} all-reduce(f32[]{:T(128)} %get-tuple-element.4), channel_id=1, replica_groups=mesh['rx'=32,'tx'=16] {'rx','tx'}, use_global_device_ids=true, to_apply=%region_5.6 | all-reduce | flops 1 | bytes 8 | tf_op jit(solution)/shard_map/psum | solution.py:79
  1089.6 0.6 multiply_add_fusion
  (24 shorter events, 0.2 us)
Async XLA Ops:
  7.2 209.1 %all-gather.4.cloned.1.call-start = ((), (), s32[]{:S(2)}) async-start(), calls=%async_computation.3 | async-start | bytes 1081344 | tf_op jit(solution)/shard_map/all_gather | solution.py:37
  7.9 331.3 %reduce-scatter.3.cloned.1.call-start = ((), (), s32[]{:S(2)}) async-start(), calls=%async_computation.4 | async-start | bytes 557056 | tf_op jit(solution)/shard_map/reduce_scatter | solution.py:57
  216.2 2.2 copy-start.1
  218.4 9.4 copy-start.3
  218.4 9.4 copy-start.4
  218.4 217.4 %reduce-scatter.5.cloned.1.call-start = ((), (), s32[]{:S(2)}) async-start(), calls=%async_computation.5 | async-start | bytes 557056 | tf_op jit(solution)/shard_map/reduce_scatter | solution.py:56
  438.0 69.4 %all-to-all-start = ((f32[16,64,128]{2,1,0:T(8,128)}), f32[16,64,128]{2,1,0:T(8,128)S(1)}, u32[]{:S(2)}, u32[]{:S(2)}) async-start(f32[16,64,128]{2,1,0:T(8,128)} %stack.2), calls=%async_computation.2 | async-start | bytes 1048576 | tf_op jit(solution)/shard_map/all_to_all | solution.py:63
  444.0 520.6 %all-reduce.2.cloned.1.call-start = ((), (), s32[]{:S(2)}) async-start(), calls=%async_computation.6 | async-start | bytes 2097152 | tf_op jit(solution)/shard_map/psum | solution.py:73
  523.7 441.0 %copy-start = (f32[64,128]{1,0:T(8,128)S(1)}, f32[64,128]{1,0:T(8,128)}, u32[]{:S(2)}) copy-start(f32[64,128]{1,0:T(8,128)} %param.8) | copy-start | bytes 98308
  966.0 124.9 %copy-start.2 = (f32[64,128]{1,0:T(8,128)}, f32[64,128]{1,0:T(8,128)S(1)}, u32[]{:S(2)}) copy-start(f32[64,128]{1,0:T(8,128)S(1)} %get-tuple-element.5) | copy-start | bytes 98308
Sparse Core Ops, SparseCore 0:
  10.1 206.1 all-gather.3
  220.9 118.3 reduce-scatter.2
  344.6 91.1 reduce-scatter.4
  523.8 440.7 all-reduce.1
